TPU v7x, 32 devices: a whole 2x2x4 slice. The times are simulated.
32 devices in a mesh: grp: 2 (over x), wide: 8 (over z, y), narrow: 2 (over core).
Axes of the slice: x: 2, y: 2, z: 4, core: 2. Of those that a mesh axis runs over, the one named last changes fastest.
Arguments:
- tokens: bfloat16 [2, 64, 8192], P(None, ('grp', 'wide'), 'narrow'), parts along dimension 1, may hold values from -6 to 6
- gate_weight: bfloat16 [8192, 26624], P('narrow', 'wide'), may hold values from -0.0625 to 0.0625
- up_weight: bfloat16 [8192, 26624], P('narrow', 'wide'), may hold values from -0.0625 to 0.0625
- down_weight: bfloat16 [26624, 8192], P('wide', 'narrow'), may hold values from -0.0390625 to 0.0390625
Outputs:
- mixed: bfloat16 [2, 64, 8192], P(None, ('grp', 'wide'), 'narrow'), parts along dimension 1
There are 2 independent parts, one for each index of `grp`. A program takes and returns all parts, laid end to end along the dimension named above; an argument that names none is the same for every part. Nothing has to cross between parts.
All inputs are finite; a program needn't handle non-finite values.
Results may differ from a plain program's by a relative error of at most 0.0075.
Values may be sent and summed in bfloat16 or wider, within the bound.
A program may use at most 256 MiB of HBM per device.

v0:
```python
import jax
import jax.numpy as jnp
from jax import lax
from jax.sharding import PartitionSpec as P


def on_device(tokens, gate_weight, up_weight, down_weight):
    units = gate_weight.shape[1]
    stacked = jnp.concatenate((gate_weight, up_weight), axis=1)
    outputs = []
    previous = None
    for step_index in range(tokens.shape[0]):
        if previous is None:
            local_rows = tokens[step_index]
        else:
            local_rows = (
                tokens[step_index].astype(jnp.float32) + previous.astype(jnp.float32)
            ).astype(jnp.bfloat16)
        partial_units = jnp.dot(
            lax.all_gather(local_rows, "wide", axis=0, tiled=True),
            stacked,
            preferred_element_type=jnp.float32,
        )
        summed = lax.psum(partial_units, "narrow")
        hidden = (jax.nn.silu(summed[:, :units]) * summed[:, units:]).astype(jnp.bfloat16)
        mixed_now = lax.psum_scatter(
            jnp.dot(hidden, down_weight, preferred_element_type=jnp.float32),
            "wide",
            scatter_dimension=0,
            tiled=True,
        ).astype(jnp.bfloat16)
        outputs.append(mixed_now)
        previous = mixed_now
    return jnp.stack(outputs)


def solution(mesh):
    in_specs = (
        P(None, ("grp", "wide"), "narrow"),
        P("narrow", "wide"),
        P("narrow", "wide"),
        P("wide", "narrow"),
    )
    out_specs = P(None, ("grp", "wide"), "narrow")
    return jax.shard_map(
        on_device, mesh=mesh, in_specs=in_specs, out_specs=out_specs, check_vma=False
    )
```

profile of v0, /device:TPU:0, one launch (start us, length us, event | category | flops | bytes accessed | tf_op | source)
XLA Modules:
  0.0 308.6 jit_solution(13444986578618834752)
XLA Ops:
  6.5 0.0 slice-start
  6.5 0.0 all-reduce.7.cloned.1.call-start
  6.5 19.4 %constant_dynamic-update-slice_fusion.1 = bf16[4096,6656]{1,0:T(8,128)(2,1)} fusion(bf16[4096,3328]{1,0:T(8,128)(2,1)} %param.5), kind=kLoop, calls=%fused_computation.20 | loop fusion | bytes 54525952
  25.9 0.0 slice-done
  26.0 0.1 copy.8
  26.0 33.0 %all-gather = bf16[1,32,4096]{2,0,1:T(2,128)(2,1)S(1)} all-gather(bf16[1,4,4096]{2,0,1:T(2,128)(2,1)S(1)} %copy.8), channel_id=2, replica_groups=mesh['grp'=2,'wide'=8,'narrow'=2] {'wide'}, dimensions={1}, use_global_device_ids=true | all-gather | bytes 294912 | tf_op jit(solution)/shard_map/all_gather | solution.py:20
  59.0 19.3 %constant_dynamic-update-slice_fusion = bf16[4096,6656]{1,0:T(8,128)(2,1)} fusion(bf16[4096,6656]{1,0:T(8,128)(2,1)} %constant_dynamic-update-slice_fusion.1, bf16[4096,3328]{1,0:T(8,128)(2,1)} %param.6), kind=kLoop, calls=%fused_computation.19 | loop fusion | bytes 54525952 | tf_op jit(solution)/shard_map/concatenate | solution.py:9
  78.3 22.3 %convolution_bitcast_fusion = f32[32,6656]{1,0:T(8,128)} fusion(bf16[4096,6656]{1,0:T(8,128)(2,1)} %constant_dynamic-update-slice_fusion, bf16[1,32,4096]{2,0,1:T(2,128)(2,1)S(1)} %all-gather), kind=kOutput, calls=%fused_computation | convolution fusion | flops 1744830464 | bytes 55640064 | tf_op jit(solution)/shard_map/dot_general | solution.py:19
  100.6 0.0 all-reduce.7.cloned.1.call-update
  100.6 0.0 all-reduce.9.cloned.1.call-start
  100.7 0.0 copy-done.1
  100.7 0.6 dynamic-slice
  101.9 19.3 %all-reduce.7.cloned.1.call-done = f32[32,6656]{1,0:T(8,128)} async-done(((f32[32,6656]{1,0:T(8,128)}), f32[32,6656]{1,0:T(8,128)}) %all-reduce.7.cloned.1.call-update) | async-done | bytes 851984 | tf_op jit(solution)/shard_map/psum | solution.py:24
  121.2 11.4 %fusion.4 = f32[32,4096]{1,0:T(8,128)S(1)} fusion(bf16[3328,4096]{1,0:T(8,128)(2,1)} %param.7, f32[32,6656]{1,0:T(8,128)} %all-reduce.7.cloned.1.call-done), kind=kOutput, calls=%fused_computation.7 | convolution fusion | flops 873054208 | bytes 28639232 | tf_op jit(solution)/shard_map/dot_general | solution.py:27
  132.6 43.6 %all-reduce.10 = bf16[32,4096]{1,0:T(8,128)(2,1)S(1)} all-reduce(f32[32,4096]{1,0:T(8,128)S(1)} %fusion.4), channel_id=3, replica_groups=mesh['grp'=2,'wide'=8,'narrow'=2] {'wide'}, use_global_device_ids=true, to_apply=%region_1.2.clone | all-reduce | flops 131072 | bytes 786432
  176.2 0.0 copy-done
  176.3 30.7 %all-gather.1 = bf16[8,4,4096]{2,1,0:T(4,128)(2,1)S(1)} all-gather(bf16[1,4,4096]{2,1,0:T(4,128)(2,1)S(1)} %fusion.12), channel_id=1, replica_groups=mesh['grp'=2,'wide'=8,'narrow'=2] {'wide'}, dimensions={0}, use_global_device_ids=true | all-gather | bytes 294912 | tf_op jit(solution)/shard_map/all_gather | solution.py:20
  207.0 0.1 reshape.5
  207.1 22.3 %fusion.16 = f32[32,6656]{1,0:T(8,128)} fusion(bf16[32,4096]{1,0:T(8,128)(2,1)S(1)} %reshape.5, bf16[4096,6656]{1,0:T(8,128)(2,1)} %constant_dynamic-update-slice_fusion), kind=kOutput, calls=%fused_computation.23 | convolution fusion | flops 1744830464 | bytes 55640064 | tf_op jit(solution)/shard_map/dot_general | solution.py:19
  229.3 0.0 all-reduce.9.cloned.1.call-update
  229.4 16.7 %all-reduce.9.cloned.1.call-done = f32[32,6656]{1,0:T(8,128)} async-done(((f32[32,6656]{1,0:T(8,128)}), f32[32,6656]{1,0:T(8,128)}) %all-reduce.9.cloned.1.call-update) | async-done | bytes 851984 | tf_op jit(solution)/shard_map/psum | solution.py:24
  246.1 11.4 %fusion.6 = f32[32,4096]{1,0:T(8,128)S(1)} fusion(bf16[3328,4096]{1,0:T(8,128)(2,1)} %param.7, f32[32,6656]{1,0:T(8,128)} %all-reduce.9.cloned.1.call-done), kind=kOutput, calls=%fused_computation.8 | convolution fusion | flops 873054208 | bytes 28639232 | tf_op jit(solution)/shard_map/dot_general | solution.py:27
  257.5 43.5 %all-reduce.11 = bf16[32,4096]{1,0:T(8,128)(2,1)S(1)} all-reduce(f32[32,4096]{1,0:T(8,128)S(1)} %fusion.6), channel_id=4, replica_groups=mesh['grp'=2,'wide'=8,'narrow'=2] {'wide'}, use_global_device_ids=true, to_apply=%region_3.4.clone | all-reduce | flops 131072 | bytes 786432
  301.0 0.7 pad_maximum_fusion
  (5 shorter events, 0.1 us)
Async XLA Ops:
  6.5 19.4 %slice-start = ((bf16[2,4,4096]{2,1,0:T(4,128)(2,1)}), bf16[1,4,4096]{2,1,0:T(4,128)(2,1)S(1)}, s32[]{:S(2)}) async-start(bf16[2,4,4096]{2,1,0:T(4,128)(2,1)} %param.4), calls=%async_computation.2 | async-start | bytes 65536 | tf_op jit(solution)/shard_map/slice | solution.py:14
  6.5 114.7 %all-reduce.7.cloned.1.call-start = ((), (), s32[]{:S(2)}) async-start(), calls=%async_computation | async-start | bytes 1703936 | tf_op jit(solution)/shard_map/psum | solution.py:24
  59.0 41.7 %copy-start.1 = (u32[32]{0:T(128)S(1)}, u32[32]{0:T(128)}, u32[]{:S(2)}) copy-start(u32[32]{0:T(128)} %constant.7) | copy-start | bytes 388
  78.3 97.9 %copy-start = (bf16[2,4,4096]{2,1,0:T(4,128)(2,1)S(1)}, bf16[2,4,4096]{2,1,0:T(4,128)(2,1)}, u32[]{:S(2)}) copy-start(bf16[2,4,4096]{2,1,0:T(4,128)(2,1)} %param.4) | copy-start | bytes 196612
  100.6 145.5 %all-reduce.9.cloned.1.call-start = ((), (), s32[]{:S(2)}) async-start(), calls=%async_computation.1 | async-start | bytes 1703936 | tf_op jit(solution)/shard_map/psum | solution.py:24
Sparse Core Ops, SparseCore 0:
  100.7 20.4 all-reduce.6
  229.5 16.5 all-reduce.8
where the time goes:
time: 309 us
  blocking collectives  151 us (49%)
  matrix products  67.4 us (22%)
  local copies, waits for them, and re-layouts  39.5 us (13%)
  waiting for transfers between devices  36 us (12%)
  between operations  14.1 us (5%)
    unnamed x2, blocking collectives  87.1 us
    all_gather x2, blocking collectives, on_device(): lax.all_gather(local_rows, 'wide', axis=0, tiled=True)  63.7 us
    dot_general x2, matrix products, on_device(): jnp.dot(lax.all_gather(local_rows, 'wide', axis=0, tiled=True), stacked,...  44.5 us
    psum x2, waiting for transfers between devices, on_device(): summed = lax.psum(partial_units, 'narrow')  36 us
    dot_general x2, matrix products, on_device(): jnp.dot(hidden, down_weight, preferred_element_type=jnp.float32)  22.8 us
    unnamed x8, local copies, waits for them, and re-layouts  20.1 us
    concatenate x1, local copies, waits for them, and re-layouts, on_device(): stacked = jnp.concatenate((gate_weight, up_weight), axis=1)  19.3 us
  transfers between devices with their start and end apart: 2, of which 2 were waited for; matrix products, arithmetic and copies ran while one was open for 0% of the time, Pallas kernels for 0%

commit v1 on v0

v1 whole, which is shorter than its diff:
```python
import functools

import jax
import jax.numpy as jnp
from jax import lax
from jax.experimental import pallas as pl
from jax.experimental.pallas import tpu as pltpu
from jax.sharding import PartitionSpec as P

F32 = jnp.float32
BF16 = jnp.bfloat16
MESH = pl.DeviceIdType.MESH
STRIP = 256
RING = 3


def kernel(
    n, groups, halves, unit_tile, tok_ref, gate_ref, up_ref, down_ref, out_ref,
    pool, tok_all, rows_in, rows_next, own_sums, send_sums, recv_sums, hidden,
    part_send, part_recv, piece, mixed_all, tail_send,
    load_sem, tok_own_sem, tok_send_sem, tok_recv_sem, pair_send_sem, pair_recv_sem,
    part_send_sem, part_recv_sem, gather_send_sem, gather_recv_sem, tail_send_sem, tail_recv_sem,
):
    steps, per_dev, width = tok_ref.shape
    units = gate_ref.shape[1]
    chunks = units // unit_tile
    strips = width // STRIP
    row_blocks = n // groups
    block_rows = per_dev * groups
    rows = n * per_dev
    me = lax.axis_index("wide")
    core = lax.axis_index("narrow")
    peer = {"narrow": 1 - core}
    my_row_block, my_group = me // groups, me % groups

    def gate_load(j):
        cols = pl.ds(pl.multiple_of(j * unit_tile, unit_tile), unit_tile)
        return [
            pltpu.make_async_copy(
                w.at[:, cols], pool.at[2 * j + i, pl.ds(0, width), pl.ds(0, unit_tile)],
                load_sem.at[2 * j + i],
            )
            for i, w in enumerate((gate_ref, up_ref))
        ]

    def strip_block(j):
        return (me + 1 + j // halves) % groups

    def down_load(j, slot):
        first = strip_block(j) * halves + j % halves
        cols = pl.ds(pl.multiple_of(first * STRIP, STRIP), STRIP)
        return pltpu.make_async_copy(
            down_ref.at[:, cols], pool.at[slot, pl.ds(0, units), pl.ds(0, STRIP)], load_sem.at[slot]
        )

    def start_gate(j, carry):
        for copy in gate_load(j):
            copy.start()
        return carry

    lax.fori_loop(0, chunks, start_gate, 0)
    for j in range(RING):
        down_load(j, 2 * chunks + j).start()

    barrier = pltpu.get_barrier_semaphore()

    def greet(i, carry):
        pl.semaphore_signal(barrier, inc=1, device_id={"wide": (me + i) % n}, device_id_type=MESH)
        return carry

    lax.fori_loop(1, n, greet, 0)
    pl.semaphore_signal(barrier, inc=1, device_id=peer, device_id_type=MESH)
    pl.semaphore_wait(barrier, n)

    def tok_copy(s, to, slot):
        return pltpu.make_async_remote_copy(
            src_ref=tok_ref.at[s], dst_ref=tok_all.at[s, slot],
            send_sem=tok_send_sem.at[s, to], recv_sem=tok_recv_sem.at[s, slot],
            device_id={"wide": to}, device_id_type=MESH,
        )

    for s in range(steps):
        own = pltpu.make_async_copy(tok_ref.at[s], tok_all.at[s, me], tok_own_sem.at[s])
        own.start()

        def send_tok(i, carry, s=s):
            tok_copy(s, (me + i) % n, me).start()
            return carry

        lax.fori_loop(1, n, send_tok, 0)

    def place_tokens(s, target):
        pltpu.make_async_copy(tok_ref.at[s], tok_all.at[s, me], tok_own_sem.at[s]).wait()

        def arrive(i, carry):
            source = (me + i) % n
            tok_copy(s, source, source).wait_recv()
            return carry

        lax.fori_loop(1, n, arrive, 0)
        per = 16 // per_dev

        def place(i, carry):
            value = jnp.concatenate(
                [tok_all[s, i * per + t].astype(F32) for t in range(per)], axis=0
            ).astype(BF16)
            at = pl.ds(pl.multiple_of(i * 16, 16), 16)
            for b in range(strips):
                target[b, at, :] = value[:, b * STRIP:(b + 1) * STRIP]
            return carry

        lax.fori_loop(0, rows // 16, place, 0)

    def pair_copy(s, j):
        return pltpu.make_async_remote_copy(
            src_ref=send_sums.at[s, j], dst_ref=recv_sums.at[s, j],
            send_sem=pair_send_sem.at[s, j], recv_sem=pair_recv_sem.at[s, j],
            device_id=peer, device_id_type=MESH,
        )

    def part_copy(s, j, r, owner, slot):
        return pltpu.make_async_remote_copy(
            src_ref=part_send.at[s, j, r],
            dst_ref=part_recv.at[s, slot, j % halves],
            send_sem=part_send_sem.at[s, j, r], recv_sem=part_recv_sem.at[s, slot, j % halves],
            device_id={"wide": owner}, device_id_type=MESH,
        )

    def gather_copy(h, to, slot):
        return pltpu.make_async_remote_copy(
            src_ref=piece.at[h], dst_ref=mixed_all.at[slot, h],
            send_sem=gather_send_sem.at[to, h], recv_sem=gather_recv_sem.at[slot, h],
            device_id={"wide": to}, device_id_type=MESH,
        )

    def tail_copy(h, t, group):
        cols = pl.ds(pl.multiple_of((group * halves + h) * STRIP, STRIP), STRIP)
        return pltpu.make_async_remote_copy(
            src_ref=tail_send.at[t, h], dst_ref=out_ref.at[1, :, cols],
            send_sem=tail_send_sem.at[t, h], recv_sem=tail_recv_sem.at[group, h],
            device_id={"wide": my_row_block * groups + t}, device_id_type=MESH,
        )

    def gate_up(s):
        def body(j, carry):
            if s == 0:
                for copy in gate_load(j):
                    copy.wait()
            x = jnp.concatenate([rows_in[b] for b in range(strips)], axis=1)
            sums = [
                jnp.dot(x, pool[2 * j + i, pl.ds(0, width), pl.ds(0, unit_tile)], preferred_element_type=F32)
                for i in range(2)
            ]
            for i in range(2):
                own_sums[j, i] = sums[i]
                send_sums[s, j, i] = sums[i].astype(BF16)
            pair_copy(s, j).start()
            if s == 1:
                for i in range(2):
                    @pl.when(2 * j + i < strips - RING)
                    def _():
                        down_load(2 * j + i, 2 * j + i).start()
            return carry

        lax.fori_loop(0, chunks, body, 0)
        def act(j, carry):
            pair_copy(s, j).wait_recv()
            gate = own_sums[j, 0] + recv_sums[s, j, 0].astype(F32)
            up = own_sums[j, 1] + recv_sums[s, j, 1].astype(F32)
            hidden[j] = (gate / (1.0 + jnp.exp(-gate)) * up).astype(BF16)
            return carry

        lax.fori_loop(0, chunks, act, 0)

    freed = min(2 * chunks, strips - RING)

    def down(s):
        def body(e, carry):
            if s == 0:
                j = e
                slot = 2 * chunks + e % RING
                down_load(j, slot).wait()
            else:
                j = (e + strips - RING) % strips
                resident = 2 * chunks + j % RING
                slot = jnp.where(e < RING, resident, (e - RING) % freed)

                @pl.when(e >= RING)
                def _():
                    down_load(j, slot).wait()

            h = jnp.concatenate([hidden[c] for c in range(chunks)], axis=1)
            part = jnp.dot(h, pool[slot, pl.ds(0, units), pl.ds(0, STRIP)], preferred_element_type=F32)
            if s == 0:
                @pl.when(e + RING < strips)
                def _():
                    down_load(e + RING, slot).start()
            elif freed < strips - RING:
                @pl.when((e >= RING) & (e + freed < strips))
                def _():
                    down_load(e - RING + freed, slot).start()
            value = part.astype(BF16)
            for rb in range(row_blocks):
                part_send[s, j, rb] = value[rb * block_rows:(rb + 1) * block_rows]
            group = strip_block(j)

            def send(r, carry):
                rb = (my_row_block + 1 + r) % row_blocks
                owner = rb * groups + group

                @pl.when(owner != me)
                def _():
                    part_copy(s, j, rb, owner, me).start()

                @pl.when(owner == me)
                def _():
                    part_recv[s, me, j % halves] = part_send[s, j, rb]

                return carry

            lax.fori_loop(0, row_blocks, send, 0)
            return carry

        lax.fori_loop(0, strips, body, 0)

    def reduce(s, h):
        def body(i, total):
            source = (me + n - i) % n
            part_copy(s, h, 0, source, source).wait_recv()
            return total + part_recv[s, source, h].astype(F32)

        return lax.fori_loop(1, n, body, part_recv[s, me, h].astype(F32))

    place_tokens(0, rows_in)
    gate_up(0)
    place_tokens(1, rows_next)
    down(0)
    for h in range(halves):
        piece[h] = reduce(0, h).astype(BF16)

        def send_piece(i, carry, h=h):
            gather_copy(h, (me + i) % n, me).start()
            return carry

        lax.fori_loop(1, n, send_piece, 0)
        mixed_all[me, h] = piece[h]

    def take(i, carry):
        source = (me + i) % n
        at = pl.ds(pl.multiple_of(source // groups * block_rows, block_rows), block_rows)
        for h in range(halves):
            @pl.when(i > 0)
            def _():
                gather_copy(h, source, source).wait_recv()

            b = source % groups * halves + h
            rows_in[b, at, :] = (
                rows_next[b, at, :].astype(F32) + mixed_all[source, h].astype(F32)
            ).astype(BF16)
        return carry

    lax.fori_loop(0, n, take, 0)

    gate_up(1)
    pick = (
        lax.broadcasted_iota(jnp.int32, (8, block_rows), 1)
        == lax.broadcasted_iota(jnp.int32, (8, block_rows), 0) + my_group * per_dev
    ).astype(F32).astype(BF16)
    for g in range(groups):
        for h in range(halves):
            mine = jnp.dot(pick, mixed_all[my_row_block * groups + g, h], preferred_element_type=F32)
            b = g * halves + h
            out_ref[0, :, b * STRIP:(b + 1) * STRIP] = mine[:per_dev].astype(BF16)
    down(1)
    for h in range(halves):
        total = reduce(1, h)
        for t in range(groups):
            tail_send[t, h] = total[t * per_dev:(t + 1) * per_dev].astype(BF16)

            @pl.when(t != my_group)
            def _():
                tail_copy(h, t, my_group).start()

        cols = pl.ds(pl.multiple_of((my_group * halves + h) * STRIP, STRIP), STRIP)
        out_ref[1, :, cols] = tail_send[my_group, h]

    for s in range(steps):
        def pair_sent(j, carry, s=s):
            pair_copy(s, j).wait_send()
            return carry

        lax.fori_loop(0, chunks, pair_sent, 0)

        def tok_sent(i, carry, s=s):
            tok_copy(s, (me + i) % n, me).wait_send()
            return carry

        lax.fori_loop(1, n, tok_sent, 0)

        def part_sent(j, carry, s=s):
            for rb in range(row_blocks):
                owner = rb * groups + strip_block(j)

                @pl.when(owner != me)
                def _():
                    part_copy(s, j, rb, owner, me).wait_send()

            return carry

        lax.fori_loop(0, strips, part_sent, 0)

    def piece_sent(i, carry):
        for h in range(halves):
            gather_copy(h, (me + i) % n, me).wait_send()
        return carry

    lax.fori_loop(1, n, piece_sent, 0)
    for h in range(halves):
        for t in range(groups):
            @pl.when(t != my_group)
            def _():
                tail_copy(h, t, my_group).wait_send()
                tail_copy(h, t, t).wait_recv()


def on_device(n, tokens, gate_weight, up_weight, down_weight):
    steps, per_dev, width = tokens.shape
    units = gate_weight.shape[1]
    unit_tile = 256 if units % 256 == 0 else units
    chunks = units // unit_tile
    groups = min(n, 8)
    halves = width // groups // STRIP
    strips = width // STRIP
    row_blocks = n // groups
    rows = n * per_dev
    block_rows = per_dev * groups
    dma = pltpu.SemaphoreType.DMA
    slots = 2 * chunks + RING
    scratch = [
        pltpu.VMEM((slots, max(width, units), max(unit_tile, STRIP)), BF16),
        pltpu.VMEM((steps, n, per_dev, width), BF16),
        pltpu.VMEM((strips, rows, STRIP), BF16),
        pltpu.VMEM((strips, rows, STRIP), BF16),
        pltpu.VMEM((chunks, 2, rows, unit_tile), F32),
        pltpu.VMEM((steps, chunks, 2, rows, unit_tile), BF16),
        pltpu.VMEM((steps, chunks, 2, rows, unit_tile), BF16),
        pltpu.VMEM((chunks, rows, unit_tile), BF16),
        pltpu.VMEM((steps, strips, row_blocks, block_rows, STRIP), BF16),
        pltpu.VMEM((steps, n, halves, block_rows, STRIP), BF16),
        pltpu.VMEM((halves, block_rows, STRIP), BF16),
        pltpu.VMEM((n, halves, block_rows, STRIP), BF16),
        pltpu.VMEM((groups, halves, per_dev, STRIP), BF16),
        dma((slots,)),
        dma((steps,)),
        dma((steps, n)),
        dma((steps, n)),
        dma((steps, chunks)),
        dma((steps, chunks)),
        dma((steps, strips, row_blocks)),
        dma((steps, n, halves)),
        dma((n, halves)),
        dma((n, halves)),
        dma((groups, halves)),
        dma((groups, halves)),
    ]
    hbm = pl.BlockSpec(memory_space=pl.ANY)
    return pl.pallas_call(
        functools.partial(kernel, n, groups, halves, unit_tile),
        out_shape=jax.ShapeDtypeStruct(tokens.shape, BF16),
        in_specs=[hbm] * 4,
        out_specs=pl.BlockSpec(memory_space=pltpu.VMEM),
        scratch_shapes=scratch,
        compiler_params=pltpu.CompilerParams(
            collective_id=0, has_side_effects=True, vmem_limit_bytes=64 * 1024 * 1024
        ),
    )(tokens, gate_weight, up_weight, down_weight)


def solution(mesh):
    in_specs = (
        P(None, ("grp", "wide"), "narrow"),
        P("narrow", "wide"),
        P("narrow", "wide"),
        P("wide", "narrow"),
    )
    return jax.shard_map(
        functools.partial(on_device, mesh.shape["wide"]),
        mesh=mesh,
        in_specs=in_specs,
        out_specs=P(None, ("grp", "wide"), "narrow"),
        check_vma=False,
    )
```

time: 309 us -> 83.2 us (0.27)
  blocking collectives: 151 us -> 0 us
  Pallas kernels: 0 us -> 81.6 us
  matrix products: 67.4 us -> 0 us
  local copies, waits for them, and re-layouts: 39.5 us -> 1.49 us
  waiting for transfers between devices: 36 us -> 0 us
  between operations: 14.1 us -> 0.01 us
    unnamed x2 -> x0, blocking collectives: 87.1 us -> none
    pallas_call x0 -> x1, Pallas kernels: none -> 81.6 us  [on_device(): pl.pallas_call(functools.partial(kernel, n, groups, halves, unit_tile), o...]
    dot_general x4 -> x0, matrix products: 67.4 us -> none  [the longest x2 44.5 us: on_device(): jnp.dot(lax.all_gather(local_rows, 'wide', axis=0, tiled=True), stacked,...]
    all_gather x2 -> x0, blocking collectives: 63.7 us -> none  [on_device(): lax.all_gather(local_rows, 'wide', axis=0, tiled=True)]
    psum x2 -> x0, waiting for transfers between devices: 36 us -> none  [on_device(): summed = lax.psum(partial_units, 'narrow')]
    concatenate x1 -> x0, local copies, waits for them, and re-layouts: 19.3 us -> none  [on_device(): stacked = jnp.concatenate((gate_weight, up_weight), axis=1)]
    unnamed x8 -> x1, local copies, waits for them, and re-layouts: 20.1 us -> 1.49 us
  transfers between devices with their start and end apart: 2 -> 0, of which waited for: 2 -> 0; matrix products, arithmetic and copies ran while one was open for 0% -> 0% of each run, Pallas kernels for 0% -> 0%
where the time goes in v1:
time: 83.2 us; the launch traced here: 83.1 us
  Pallas kernels  81.6 us (98%)
  local copies, waits for them, and re-layouts  1.49 us (2%)
    pallas_call x1, Pallas kernels, on_device(): pl.pallas_call(functools.partial(kernel, n, groups, halves, unit_tile), o...  81.6 us

profile of v1, /device:TPU:0, one launch (start us, length us, event | category | flops | bytes accessed | tf_op | source)
XLA Modules:
  0.0 83.1 jit_solution(6758705398099762444)
XLA Ops:
  0.0 81.6 %shard_map.46 = bf16[2,4,4096]{2,1,0:T(4,128)(2,1)} custom-call(bf16[2,4,4096]{2,1,0:T(4,128)(2,1)} %tok_ref.1, bf16[4096,3328]{1,0:T(8,128)(2,1)} %gate_ref.1, bf16[4096,3328]{1,0:T(8,128)(2,1)} %up_ref.1, bf16[3328,4096]{1,0:T(8,128)(2,1)} %down_ref.1), custom_call_target="tpu_custom_call" | custom-call | tf_op jit(solution)/shard_map/pallas_call | solution.py:367
  81.6 1.5 %copy.6 = bf16[2,4,4096]{2,1,0:T(4,128)(2,1)} copy(bf16[2,4,4096]{2,1,0:T(4,128)(2,1)} %shard_map.46) | data formatting | bytes 131072

commit v2 on v0

v2 whole, which is shorter than its diff:
```python
import functools

import jax
import jax.numpy as jnp
from jax import lax
from jax.experimental import pallas as pl
from jax.experimental.pallas import tpu as pltpu
from jax.sharding import PartitionSpec as P

F32 = jnp.float32
BF16 = jnp.bfloat16
MESH = pl.DeviceIdType.MESH
STRIP = 256
AHEAD = 4
LAG = (3, 8)
QUARTERS = 4
RING = 4


def kernel(
    n, unit_tile, tok_ref, gate_ref, up_ref, down_ref, out_ref,
    pool, ring, tok_all, tok_next, rows_in, own_sums, send_sums, recv_sums, hidden,
    part_send, part_recv, rows_all,
    load_sem, ring_sem, tok_own_sem, tok_send_sem, tok_recv_sem, pair_send_sem, pair_recv_sem,
    part_send_sem, part_recv_sem, gather_send_sem, gather_recv_sem,
):
    steps, per_dev, width = tok_ref.shape
    units = gate_ref.shape[1]
    chunks = units // unit_tile
    strips = width // STRIP
    per_quarter = strips // QUARTERS
    span = width // QUARTERS
    rows = n * per_dev
    me = lax.axis_index("wide")
    core = lax.axis_index("narrow")
    peer = {"narrow": 1 - core}

    def gate_load(j):
        cols = pl.ds(pl.multiple_of(j * unit_tile, unit_tile), unit_tile)
        return [
            pltpu.make_async_copy(
                w.at[:, cols], pool.at[2 * j + i, pl.ds(0, width), pl.ds(0, unit_tile)],
                load_sem.at[2 * j + i],
            )
            for i, w in enumerate((gate_ref, up_ref))
        ]

    def down_load(j, slot):
        cols = pl.ds(pl.multiple_of(j * STRIP, STRIP), STRIP)
        return pltpu.make_async_copy(
            down_ref.at[:, cols], pool.at[slot, pl.ds(0, units), pl.ds(0, STRIP)], load_sem.at[slot]
        )

    def ring_load(j):
        cols = pl.ds(pl.multiple_of(j * STRIP, STRIP), STRIP)
        return pltpu.make_async_copy(down_ref.at[:, cols], ring.at[j % RING], ring_sem.at[j % RING])

    ahead = min(AHEAD, chunks)
    early = min(3, chunks)

    def start_gate(j, carry):
        for copy in gate_load(j):
            copy.start()
        return carry

    def loaded(j, carry):
        for copy in gate_load(j):
            copy.wait()
        later = j + ahead

        @pl.when(later < chunks)
        def _():
            start_gate(later, 0)

        @pl.when((later >= chunks) & (later < chunks + RING))
        def _():
            ring_load(later - chunks).start()

        return carry

    lax.fori_loop(0, ahead, start_gate, 0)

    barrier = pltpu.get_barrier_semaphore()

    def greet(i, carry):
        pl.semaphore_signal(barrier, inc=1, device_id={"wide": (me + i) % n}, device_id_type=MESH)
        return carry

    lax.fori_loop(1, n, greet, 0)
    pl.semaphore_signal(barrier, inc=1, device_id=peer, device_id_type=MESH)
    pl.semaphore_wait(barrier, n)

    def tok_copy(to, slot):
        return pltpu.make_async_remote_copy(
            src_ref=tok_ref.at[0], dst_ref=tok_all.at[slot],
            send_sem=tok_send_sem.at[to], recv_sem=tok_recv_sem.at[slot],
            device_id={"wide": to}, device_id_type=MESH,
        )

    def others(act):
        def one(i, carry):
            act((me + i) % n)
            return carry

        lax.fori_loop(1, n, one, 0)

    own_tokens = [
        pltpu.make_async_copy(tok_ref.at[0], tok_all.at[me], tok_own_sem.at[0]),
        pltpu.make_async_copy(tok_ref.at[1], tok_next, tok_own_sem.at[1]),
    ]

    def place(read, first):
        per = 16 // per_dev

        def one(i, carry):
            value = jnp.concatenate(
                [read(i * per + t).astype(F32) for t in range(per)], axis=0
            ).astype(BF16)
            at = pl.ds(pl.multiple_of(i * 16, 16), 16)
            for b in range(value.shape[1] // STRIP):
                rows_in[first + b, at, :] = value[:, b * STRIP:(b + 1) * STRIP]
            return carry

        lax.fori_loop(0, rows // 16, one, 0)

    def pair_copy(s, j):
        return pltpu.make_async_remote_copy(
            src_ref=send_sums.at[s, j], dst_ref=recv_sums.at[s, j],
            send_sem=pair_send_sem.at[s, j], recv_sem=pair_recv_sem.at[s, j],
            device_id=peer, device_id_type=MESH,
        )

    def part_copy(s, q, owner, slot):
        return pltpu.make_async_remote_copy(
            src_ref=part_send.at[s, q, owner], dst_ref=part_recv.at[s, q, slot],
            send_sem=part_send_sem.at[s, q, owner], recv_sem=part_recv_sem.at[s, q, slot],
            device_id={"wide": owner}, device_id_type=MESH,
        )

    def gather_copy(q, to, slot):
        return pltpu.make_async_remote_copy(
            src_ref=rows_all.at[q, me], dst_ref=rows_all.at[q, slot],
            send_sem=gather_send_sem.at[q, to], recv_sem=gather_recv_sem.at[q, slot],
            device_id={"wide": to}, device_id_type=MESH,
        )

    def gate_up_part(q):
        def tile(j):
            x = jnp.concatenate([rows_in[q * per_quarter + b] for b in range(per_quarter)], axis=1)
            for i in range(2):
                value = jnp.dot(
                    x, pool[2 * j + i, pl.ds(q * span, span), pl.ds(0, unit_tile)],
                    preferred_element_type=F32,
                )
                own_sums[j, i] = value if q == 0 else own_sums[j, i] + value

        def body(p, carry):
            for k in range(4):
                tile(4 * p + k)
            return carry

        lax.fori_loop(0, chunks // 4, body, 0)
        for j in range(chunks // 4 * 4, chunks):
            tile(j)

    def gate_up(s):
        skip = 0 if s == 0 else QUARTERS - 1

        lag = min(LAG[s], chunks)

        def act(j):
            gate = own_sums[j, 0] + recv_sums[s, j, 0].astype(F32)
            up = own_sums[j, 1] + recv_sums[s, j, 1].astype(F32)
            hidden[j] = (gate / (1.0 + jnp.exp(-gate)) * up).astype(BF16)

        def body(j, carry, active):
            if s == 0:
                @pl.when(j >= early)
                def _():
                    loaded(j, 0)
            if active:
                pair_copy(s, j - lag).wait_recv()
                act(j - lag)
            x = jnp.concatenate([rows_in[b] for b in range(skip * per_quarter, strips)], axis=1)
            sums = [
                jnp.dot(
                    x, pool[2 * j + i, pl.ds(skip * span, width - skip * span), pl.ds(0, unit_tile)],
                    preferred_element_type=F32,
                )
                for i in range(2)
            ]
            if skip:
                sums = [own_sums[j, i] + sums[i] for i in range(2)]
            for i in range(2):
                own_sums[j, i] = sums[i]
                send_sums[s, j, i] = sums[i].astype(BF16)
            pair_copy(s, j).start()
            if s == 1:
                for i in range(2):
                    @pl.when(2 * j + i < strips - RING)
                    def _():
                        down_load(2 * j + i, 2 * j + i).start()
            return carry

        lax.fori_loop(0, lag, functools.partial(body, active=False), 0)
        if chunks > lag:
            lax.fori_loop(lag, chunks, functools.partial(body, active=True), 0)
        if s == 0:
            for d in range(ahead, RING):
                ring_load(d).start()
        for j in range(chunks - lag, chunks):
            pair_copy(s, j).wait_recv()
            act(j)

    freed = min(2 * chunks, strips - RING)

    def down(s):
        def two(p, first, strip_of, started):
            h = jnp.concatenate([hidden[c] for c in range(chunks)], axis=1)
            strip = [first + 2 * p + i for i in range(2)]
            parts = [jnp.dot(h, strip_of(j), preferred_element_type=F32) for j in strip]
            for j in strip:
                started(j)
            q = strip[0] // per_quarter
            for j, part in zip(strip, parts):
                at = pl.ds(pl.multiple_of(j % per_quarter * STRIP, STRIP), STRIP)
                for d in range(n):
                    part_send[s, q, d, :, at] = part[d * per_dev:(d + 1) * per_dev].astype(BF16)

            @pl.when(p % (per_quarter // 2) == per_quarter // 2 - 1)
            def _():
                others(lambda to: part_copy(s, q, to, me).start())

        def through_ring(p, carry):
            for i in range(2):
                ring_load(2 * p + i).wait()

            def more(j):
                @pl.when(j + RING < strips)
                def _():
                    ring_load(j + RING).start()

            two(p, 0, lambda j: ring[j % RING], more)
            return carry

        def from_ring(p, carry):
            two(p, strips - RING, lambda j: ring[j % RING], lambda j: None)
            return carry

        def from_pool(p, carry):
            for i in range(2):
                down_load(2 * p + i, (2 * p + i) % freed).wait()

            def more(j):
                if freed < strips - RING:
                    @pl.when(j + freed < strips - RING)
                    def _():
                        down_load(j + freed, j % freed).start()

            two(p, 0, lambda j: pool[j % freed, pl.ds(0, units), pl.ds(0, STRIP)], more)
            return carry

        if s == 0:
            lax.fori_loop(0, strips // 2, through_ring, 0)
        else:
            lax.fori_loop(0, RING // 2, from_ring, 0)
            lax.fori_loop(0, (strips - RING) // 2, from_pool, 0)

    def reduce(s, q):
        def body(i, total):
            source = (me + i) % n
            part_copy(s, q, source, source).wait_recv()
            return total + part_recv[s, q, source].astype(F32)

        mixed = lax.fori_loop(1, n, body, part_send[s, q, me].astype(F32)).astype(BF16)
        out_ref[s, :, q * span:(q + 1) * span] = mixed
        return mixed

    for copy in own_tokens:
        copy.start()
    others(lambda to: tok_copy(to, me).start())
    lax.fori_loop(0, early, loaded, 0)
    for copy in own_tokens:
        copy.wait()
    others(lambda source: tok_copy(source, source).wait_recv())
    place(lambda i: tok_all[i], 0)
    gate_up(0)
    down(0)

    def hand_on(q):
        mixed = reduce(0, q)
        new = tok_next[:, q * span:(q + 1) * span].astype(F32)
        rows_all[q, me] = (new + mixed.astype(F32)).astype(BF16)
        others(lambda to: gather_copy(q, to, me).start())

    def take(q):
        others(lambda source: gather_copy(q, source, source).wait_recv())
        place(lambda i: rows_all[q, i], q * per_quarter)

    for q in range(QUARTERS - 1):
        hand_on(q)

    for q in range(QUARTERS - 1):
        take(q)
        gate_up_part(q)
        if q == 0:
            hand_on(QUARTERS - 1)
    take(QUARTERS - 1)
    gate_up(1)
    down(1)
    for q in range(QUARTERS):
        reduce(1, (q + QUARTERS - 1) % QUARTERS)

    for s in range(steps):
        def pair_sent(j, carry, s=s):
            pair_copy(s, j).wait_send()
            return carry

        lax.fori_loop(0, chunks, pair_sent, 0)

        for q in range(QUARTERS):
            others(lambda to: part_copy(s, q, to, me).wait_send())
    others(lambda to: tok_copy(to, me).wait_send())
    for q in range(QUARTERS):
        others(lambda to: gather_copy(q, to, me).wait_send())


def on_device(n, tokens, gate_weight, up_weight, down_weight):
    steps, per_dev, width = tokens.shape
    units = gate_weight.shape[1]
    unit_tile = 256 if units % 256 == 0 else units
    chunks = units // unit_tile
    groups = min(n, 8)
    strips = width // STRIP
    rows = n * per_dev
    span = width // QUARTERS
    dma = pltpu.SemaphoreType.DMA
    slots = 2 * chunks
    scratch = [
        pltpu.VMEM((slots, max(width, units), max(unit_tile, STRIP)), BF16),
        pltpu.VMEM((RING, units, STRIP), BF16),
        pltpu.VMEM((n, per_dev, width), BF16),
        pltpu.VMEM((per_dev, width), BF16),
        pltpu.VMEM((strips, rows, STRIP), BF16),
        pltpu.VMEM((chunks, 2, rows, unit_tile), F32),
        pltpu.VMEM((steps, chunks, 2, rows, unit_tile), BF16),
        pltpu.VMEM((steps, chunks, 2, rows, unit_tile), BF16),
        pltpu.VMEM((chunks, rows, unit_tile), BF16),
        pltpu.VMEM((steps, QUARTERS, n, per_dev, span), BF16),
        pltpu.VMEM((steps, QUARTERS, n, per_dev, span), BF16),
        pltpu.VMEM((QUARTERS, n, per_dev, span), BF16),
        dma((slots,)),
        dma((RING,)),
        dma((2,)),
        dma((n,)),
        dma((n,)),
        dma((steps, chunks)),
        dma((steps, chunks)),
        dma((steps, QUARTERS, n)),
        dma((steps, QUARTERS, n)),
        dma((QUARTERS, n)),
        dma((QUARTERS, n)),
    ]
    hbm = pl.BlockSpec(memory_space=pl.ANY)
    return pl.pallas_call(
        functools.partial(kernel, n, unit_tile),
        out_shape=jax.ShapeDtypeStruct(tokens.shape, BF16),
        in_specs=[hbm] * 4,
        out_specs=pl.BlockSpec(memory_space=pltpu.VMEM),
        scratch_shapes=scratch,
        compiler_params=pltpu.CompilerParams(
            collective_id=0, has_side_effects=True, vmem_limit_bytes=64 * 1024 * 1024
        ),
    )(tokens, gate_weight, up_weight, down_weight)


def solution(mesh):
    in_specs = (
        P(None, ("grp", "wide"), "narrow"),
        P("narrow", "wide"),
        P("narrow", "wide"),
        P("wide", "narrow"),
    )
    return jax.shard_map(
        functools.partial(on_device, mesh.shape["wide"]),
        mesh=mesh,
        in_specs=in_specs,
        out_specs=P(None, ("grp", "wide"), "narrow"),
        check_vma=False,
    )
```

time: 309 us -> 71.9 us (0.23)
  blocking collectives: 151 us -> 0 us
  Pallas kernels: 0 us -> 70.2 us
  matrix products: 67.4 us -> 0 us
  local copies, waits for them, and re-layouts: 39.5 us -> 1.49 us
  waiting for transfers between devices: 36 us -> 0 us
  between operations: 14.1 us -> 0.01 us
    unnamed x2 -> x0, blocking collectives: 87.1 us -> none
    pallas_call x0 -> x1, Pallas kernels: none -> 70.2 us  [on_device(): pl.pallas_call(functools.partial(kernel, n, unit_tile), out_shape=jax.Sha...]
    dot_general x4 -> x0, matrix products: 67.4 us -> none  [the longest x2 44.5 us: on_device(): jnp.dot(lax.all_gather(local_rows, 'wide', axis=0, tiled=True), stacked,...]
    all_gather x2 -> x0, blocking collectives: 63.7 us -> none  [on_device(): lax.all_gather(local_rows, 'wide', axis=0, tiled=True)]
    psum x2 -> x0, waiting for transfers between devices: 36 us -> none  [on_device(): summed = lax.psum(partial_units, 'narrow')]
    concatenate x1 -> x0, local copies, waits for them, and re-layouts: 19.3 us -> none  [on_device(): stacked = jnp.concatenate((gate_weight, up_weight), axis=1)]
    unnamed x8 -> x1, local copies, waits for them, and re-layouts: 20.1 us -> 1.49 us
  transfers between devices with their start and end apart: 2 -> 0, of which waited for: 2 -> 0; matrix products, arithmetic and copies ran while one was open for 0% -> 0% of each run, Pallas kernels for 0% -> 0%
where the time goes in v2:
time: 71.9 us; the launch traced here: 71.7 us
  Pallas kernels  70.2 us (98%)
  local copies, waits for them, and re-layouts  1.49 us (2%)
    pallas_call x1, Pallas kernels, on_device(): pl.pallas_call(functools.partial(kernel, n, unit_tile), out_shape=jax.Sha...  70.2 us
    unnamed x1, local copies, waits for them, and re-layouts  1.49 us

profile of v2, /device:TPU:0, one launch (start us, length us, event | category | flops | bytes accessed | tf_op | source)
XLA Modules:
  0.0 71.7 jit_solution(8126185216939217241)
XLA Ops:
  0.0 70.2 %shard_map.46 = bf16[2,4,4096]{2,1,0:T(4,128)(2,1)} custom-call(bf16[2,4,4096]{2,1,0:T(4,128)(2,1)} %tok_ref.1, bf16[4096,3328]{1,0:T(8,128)(2,1)} %gate_ref.1, bf16[4096,3328]{1,0:T(8,128)(2,1)} %up_ref.1, bf16[3328,4096]{1,0:T(8,128)(2,1)} %down_ref.1), custom_call_target="tpu_custom_call" | custom-call | tf_op jit(solution)/shard_map/pallas_call | solution.py:365
  70.2 1.5 %copy.6 = bf16[2,4,4096]{2,1,0:T(4,128)(2,1)} copy(bf16[2,4,4096]{2,1,0:T(4,128)(2,1)} %shard_map.46) | data formatting | bytes 131072
